TPU v7x, 128 devices: a whole 4x4x4 slice. The times are simulated.
128 devices in a mesh: gx: 4 (over y_lo, core), gy: 4 (over z), gz: 8 (over y_hi, x).
Axes of the slice: x: 4, y: 4 (y_hi: 2, y_lo: 2; y = y_hi * 2 + y_lo), z: 4, core: 2. Of those that a mesh axis runs over, the one named last changes fastest.
Arguments:
- right_sides: float32 [6, 128, 128, 1024], P(None, 'gx', 'gy', 'gz'), may hold values from -6 to 6
- permeability: float32 [128, 128, 1024], P('gx', 'gy', 'gz'), may hold values from 0.1 to 10
Outputs:
- basis_q: float32 [24, 128, 128, 1024], P(None, 'gx', 'gy', 'gz')
- factor_r: float32 [24, 24], replicated
All inputs are finite; a program needn't handle non-finite values.
Results may differ from a plain program's by a relative error of at most 0.00012.
Values sent between devices are 32-bit elements; how exact they have to be, the bound alone decides.
A program may use at most 128 MiB of HBM per device.

v0:
```python
import jax
import jax.numpy as jnp
from jax import lax
from jax.sharding import PartitionSpec as P


def extended(cells, sides, width):
    for axis, dim in sides:
        count = lax.axis_size(axis)
        ends = count - 1
        head = lax.slice_in_dim(cells, 0, width, axis=dim)
        tail = lax.slice_in_dim(cells, cells.shape[dim] - width, cells.shape[dim], axis=dim)
        cells = jnp.concatenate(
            [
                lax.ppermute(tail, axis, [(i, (i + 1) % count) for i in range(ends)]),
                cells,
                lax.ppermute(head, axis, [((i + 1) % count, i) for i in range(ends)]),
            ],
            axis=dim,
        )
    return cells


def face_weights(kappa_pad):
    center = kappa_pad[1:-1, 1:-1, 1:-1]
    others = [
        kappa_pad[2:, 1:-1, 1:-1],
        kappa_pad[:-2, 1:-1, 1:-1],
        kappa_pad[1:-1, 2:, 1:-1],
        kappa_pad[1:-1, :-2, 1:-1],
        kappa_pad[1:-1, 1:-1, 2:],
        kappa_pad[1:-1, 1:-1, :-2],
    ]
    face_list = []
    for neighbour in others:
        divisor = center + neighbour
        divisor = jnp.where(divisor > 0, divisor, 1.0)
        face_list.append(2.0 * center * neighbour / divisor)
    diagonal = face_list[0]
    for weight in face_list[1:]:
        diagonal = diagonal + weight
    diagonal = jnp.where(diagonal > 0, diagonal, 1.0)
    return (face_list, diagonal)


def stencil(field_pad, face_list, diagonal):
    slices = [
        field_pad[:, 2:, 1:-1, 1:-1],
        field_pad[:, :-2, 1:-1, 1:-1],
        field_pad[:, 1:-1, 2:, 1:-1],
        field_pad[:, 1:-1, :-2, 1:-1],
        field_pad[:, 1:-1, 1:-1, 2:],
        field_pad[:, 1:-1, 1:-1, :-2],
    ]
    accum = face_list[0] * slices[0]
    for weight, piece in zip(face_list[1:], slices[1:]):
        accum = accum + weight * piece
    return 2.5 * accum / diagonal


def lower_factor(matrix):
    order = matrix.shape[0]
    positions = jnp.arange(order)
    lower = jnp.zeros_like(matrix)
    for column in range(order):
        remain = matrix[:, column] - jnp.dot(lower, lower[column], precision=lax.Precision.HIGHEST)
        pivot = jnp.sqrt(remain[column])
        entries = jnp.where(
            positions > column, remain / pivot, jnp.where(positions == column, pivot, 0.0)
        )
        lower = lower + entries[:, None] * (positions[None, :] == column).astype(matrix.dtype)
    return lower


def lower_inverse(lower):
    order = lower.shape[0]
    positions = jnp.arange(order)
    inverse = jnp.zeros_like(lower)
    for row_index in range(order):
        unit_row = (positions == row_index).astype(lower.dtype)
        partial_row = unit_row - jnp.dot(lower[row_index], inverse, precision=lax.Precision.HIGHEST)
        new_row = partial_row / lower[row_index, row_index]
        inverse = inverse + unit_row[:, None] * new_row[None, :]
    return inverse


def on_device(right_sides, permeability):
    depth = 3
    powers = [right_sides]
    kappa_pad = extended(permeability, (("gx", 0), ("gy", 1), ("gz", 2)), 1)
    face_list, diagonal = face_weights(kappa_pad)
    field = right_sides
    for power_index in range(depth):
        padded = extended(field, (("gx", 1), ("gy", 2), ("gz", 3)), 1)
        field = stencil(padded, face_list, diagonal)
        powers.append(field)
    basis = jnp.concatenate(powers, 0)
    columns = basis.shape[0]
    flat = basis.reshape(columns, -1)
    cell_count = flat.shape[1] * lax.axis_size("gx") * lax.axis_size("gy") * lax.axis_size("gz")
    gram = jnp.dot(flat, flat.T, precision=lax.Precision.HIGHEST)
    total_gram = lax.psum(gram, ("gx", "gy", "gz"))
    factor_r = lower_factor(total_gram / cell_count).T
    inverse = lower_inverse(factor_r.T)
    solved = jnp.dot(inverse, flat, precision=lax.Precision.HIGHEST)
    return (solved.reshape(basis.shape), factor_r)


def solution(mesh):
    placed = (P(None, "gx", "gy", "gz"), P("gx", "gy", "gz"))
    return jax.shard_map(
        on_device,
        mesh=mesh,
        in_specs=placed,
        out_specs=(P(None, "gx", "gy", "gz"), P()),
        check_vma=False,
    )
```

profile of v0, /device:TPU:1, one launch (start us, length us, event | category | flops | bytes accessed | tf_op | source)
XLA Modules:
  0.0 477.7 jit_solution(12275474916651257987)
XLA Ops:
  1.4 4.6 collective-permute-start.2
  8.0 4.7 copy.166
  56.0 5.2 %fusion.259 = (f32[6,34,34,1]{3,0,2,1:T(8,128)}, f32[6,34,34,1]{3,0,2,1:T(8,128)}) fusion(f32[6,34,34,128]{3,0,2,1:T(8,128)S(1)} %pad_maximum_fusion.1), kind=kLoop, calls=%fused_computation.574 | loop fusion | bytes 110976 | tf_op jit(solution)/shard_map/slice | solution.py:11
  70.4 4.8 collective-permute-start.11
  75.2 4.7 compare_select_fusion
  88.6 15.8 %fusion.31 = f32[6,32,32,128]{3,0,2,1:T(8,128)S(1)} fusion(f32[6,34,34,1]{3,0,2,1:T(8,128)} %copy.157, f32[6,34,1,128]{3,0,2,1:T(8,128)S(1)} %collective-permute-done.5, f32[6,34,32,128]{3,0,2,1:T(8,128)} %copy-done.6, f32[6,34,1,128]{3,0,2,1:T(8,128)S(1)} %collective-permute-done.7, f32[6,34,34,1]{3,0,2,1:T(8,128)} %copy.153, ...), kind=kLoop, calls=%fused_computation.73 | loop fusion | flops 18087936 | bytes 13764800 | tf_op jit(solution)/shard_map/div | solution.py:58
  107.7 4.9 %collective-permute-start.13 = (f32[6,1,32,128]{3,0,2,1:T(8,128)S(1)}, f32[6,1,32,128]{3,0,2,1:T(8,128)S(1)}, u32[]{:S(2)}, u32[]{:S(2)}) collective-permute-start(f32[6,1,32,128]{3,0,2,1:T(8,128)S(1)} %get-tuple-element.59), channel_id=1, source_target_pairs={{0,32},{32,64},{64,96},{1,33},{33,65},{65,97},{2,34},{34,66},{66,9... | collective-permute-start | bytes 294920 | tf_op jit(solution)/shard_map/ppermute | solution.py:15
  123.2 5.2 %fusion.258 = (f32[6,34,34,1]{3,0,2,1:T(8,128)}, f32[6,34,34,1]{3,0,2,1:T(8,128)}) fusion(f32[6,34,34,128]{3,0,2,1:T(8,128)S(1)} %pad_maximum_fusion.2), kind=kLoop, calls=%fused_computation.573 | loop fusion | bytes 110976 | tf_op jit(solution)/shard_map/slice | solution.py:11
  136.9 4.8 %collective-permute-start.17 = (f32[6,34,34,1]{2,3,1,0:T(1,128)}, f32[6,34,34,1]{2,3,1,0:T(1,128)}, u32[]{:S(2)}, u32[]{:S(2)}) collective-permute-start(f32[6,34,34,1]{2,3,1,0:T(1,128)} %copy.160), channel_id=1, source_target_pairs={{0,1},{1,2},{2,3},{3,4},{4,5},{5,6},{6,7},{8,9},{9,10},{10,11},{11... | collective-permute-start | bytes 83240 | tf_op jit(solution)/shard_map/ppermute | solution.py:15
  151.0 18.5 %fusion.18 = f32[6,32,32,128]{3,0,2,1:T(8,128)S(1)} fusion(f32[6,34,34,1]{3,0,2,1:T(8,128)} %copy.161, f32[6,34,1,128]{3,0,2,1:T(8,128)} %copy-done.14, f32[6,34,1,128]{3,0,2,1:T(8,128)} %copy-done.16, f32[6,1,32,128]{3,0,2,1:T(8,128)S(1)} %collective-permute-done.12, f32[6,32,32,128]{3,0,2,1:T(8,128)} %copy-done.1, ...), kind=kLoop, calls=%fused_computation.42 | loop fusion | flops 24379392 | bytes 10422464 | tf_op jit(solution)/shard_map/div | solution.py:58
  171.4 5.8 %collective-permute-start.19 = (f32[6,1,32,128]{3,0,2,1:T(8,128)S(1)}, f32[6,1,32,128]{3,0,2,1:T(8,128)S(1)}, u32[]{:S(2)}, u32[]{:S(2)}) collective-permute-start(f32[6,1,32,128]{3,0,2,1:T(8,128)S(1)} %get-tuple-element.57), channel_id=1, source_target_pairs={{0,32},{32,64},{64,96},{1,33},{33,65},{65,97},{2,34},{34,66},{66,9... | collective-permute-start | bytes 294920 | tf_op jit(solution)/shard_map/ppermute | solution.py:15
  180.5 4.7 collective-permute-start.21
  188.3 5.2 %fusion.257 = (f32[6,34,34,1]{3,0,2,1:T(8,128)}, f32[6,34,34,1]{3,0,2,1:T(8,128)}) fusion(f32[6,34,34,128]{3,0,2,1:T(8,128)S(1)} %pad_maximum_fusion.3), kind=kLoop, calls=%fused_computation.572 | loop fusion | bytes 110976 | tf_op jit(solution)/shard_map/slice | solution.py:11
  201.4 4.8 %collective-permute-start.23 = (f32[6,34,34,1]{2,3,1,0:T(1,128)S(1)}, f32[6,34,34,1]{2,3,1,0:T(1,128)S(1)}, u32[]{:S(2)}, u32[]{:S(2)}) collective-permute-start(f32[6,34,34,1]{2,3,1,0:T(1,128)S(1)} %copy.164), channel_id=1, source_target_pairs={{0,1},{1,2},{2,3},{3,4},{4,5},{5,6},{6,7},{8,9},{9,10},{10,11},{11... | collective-permute-start | bytes 83240 | tf_op jit(solution)/shard_map/ppermute | solution.py:15
  213.9 19.3 %fusion.5 = f32[6,32,32,128]{3,0,2,1:T(8,128)} fusion(f32[6,34,34,1]{3,0,2,1:T(8,128)} %copy.165, f32[6,34,1,128]{3,0,2,1:T(8,128)} %copy-done.13, f32[6,34,1,128]{3,0,2,1:T(8,128)} %copy-done.15, f32[6,1,32,128]{3,0,2,1:T(8,128)} %copy-done.11, f32[6,32,32,128]{3,0,2,1:T(8,128)} %copy-done.3, f32[6,1,32,128]{3,0,2,1:T(8,128)} %copy-done.12, ...), kind=kLoop, calls=%fused_computation.11 | loop fusion | flops 24379392 | bytes 10422464 | tf_op jit(solution)/shard_map/div | solution.py:58
  233.2 6.2 %pad_maximum_fusion = f32[24,32,32,128]{3,0,2,1:T(8,128)S(1)} fusion(f32[6,32,32,128]{3,0,2,1:T(8,128)} %fusion.5, f32[6,32,32,128]{3,0,2,1:T(8,128)S(1)} %copy-done.4, f32[6,32,32,128]{3,0,2,1:T(8,128)S(1)} %copy-done.2, f32[6,32,32,128]{3,0,2,1:T(8,128)} %copy-done.5), kind=kLoop, calls=%fused_computation.1 | loop fusion | flops 9437184 | bytes 25165824 | tf_op jit(solution)/shard_map/concatenate | solution.py:97
  239.5 4.8 copy-done
  244.4 13.1 %convolution_bitcast_fusion = f32[24,24]{1,0:T(8,128)S(1)} fusion(f32[24,32,32,128]{3,0,2,1:T(8,128)S(1)} %pad_maximum_fusion), kind=kOutput, calls=%fused_computation.99 | convolution fusion | flops 905969664 | bytes 12585216 | tf_op jit(solution)/shard_map/dot_general | solution.py:101
  257.5 83.5 %psum.7 = f32[24,24]{1,0:T(8,128)S(1)} all-reduce(f32[24,24]{1,0:T(8,128)S(1)} %convolution_bitcast_fusion), channel_id=1, replica_groups=mesh['gx'=4,'gy'=4,'gz'=8] {'gx','gy','gz'}, use_global_device_ids=true, to_apply=%region_0.1 | all-reduce | flops 576 | bytes 4608 | tf_op jit(solution)/shard_map/psum | solution.py:102
  381.4 11.5 %copy.167 = f32[24,32,32,128]{3,2,1,0:T(8,128)} copy(f32[24,32,32,128]{3,0,2,1:T(8,128)} %copy-done) | data formatting | bytes 25165824 | tf_op jit(solution)/shard_map/concatenate | solution.py:97
  409.7 16.8 %copy.180 = f32[3,8,1024,128]{3,1,2,0:T(8,128)} copy(f32[3,8,1024,128]{3,2,1,0:T(8,128)} %bitcast.525) | data formatting | bytes 25165824
  426.5 11.3 %copy.175 = f32[3,8,1024,128]{3,2,1,0:T(8,128)} copy(f32[3,8,1024,128]{3,1,2,0:T(8,128)} %copy.180) | data formatting | bytes 25165824
  441.0 24.5 %fusion = f32[24,32,32,128]{3,0,2,1:T(8,128)} fusion(f32[32,32,128,24]{2,1,0,3:T(8,128)} %bitcast.526, f32[24,24]{1,0:T(8,128)S(1)} %multiply_add_fusion.5, f32[24]{0:T(128)S(1)} %fusion.112, f32[24]{0:T(128)S(1)} %copy-done.44, f32[24]{0:T(128)S(1)} %fusion.111, f32[24]{0:T(128)S(1)} %copy-done.43, f32[24]{0:T(128)S(1)} %fusion.110, f32[24]{0:T(128)S(1)} %copy-done.42, ...), kind=kOutput, calls=%fused_computation.2 | convolution fusion | flops 905974272 | bytes 25168896 | tf_op jit(solution)/shard_map/dot_general | solution.py:105
  465.5 11.8 %copy.169 = f32[24,32,32,128]{3,2,1,0:T(8,128)} copy(f32[24,32,32,128]{3,0,2,1:T(8,128)} %fusion) | data formatting | bytes 25165824
  (310 shorter events, 163.1 us)
Async XLA Ops:
  1.4 20.9 %collective-permute-start.2 = (f32[1,32,128]{2,1,0:T(8,128)S(1)}, f32[1,32,128]{2,1,0:T(8,128)S(1)}, u32[]{:S(2)}, u32[]{:S(2)}) collective-permute-start(f32[1,32,128]{2,1,0:T(8,128)S(1)} %get-tuple-element.68), channel_id=1, source_target_pairs={{0,32},{32,64},{64,96},{1,33},{33,65},{65,97},{2,34},{34,66},{66,9... | collective-permute-start | bytes 49160 | tf_op jit(solution)/shard_map/ppermute | solution.py:15
  6.0 16.3 %collective-permute-start = (f32[1,32,128]{2,1,0:T(8,128)S(1)}, f32[1,32,128]{2,1,0:T(8,128)S(1)}, u32[]{:S(2)}, u32[]{:S(2)}) collective-permute-start(f32[1,32,128]{2,1,0:T(8,128)S(1)} %get-tuple-element.67), channel_id=1, source_target_pairs={{32,0},{64,32},{96,64},{33,1},{65,33},{97,65},{34,2},{66,34},{98,6... | collective-permute-start | bytes 49160 | tf_op jit(solution)/shard_map/ppermute | solution.py:17
  15.4 24.2 %collective-permute-start.3 = (f32[6,1,32,128]{3,0,2,1:T(8,128)}, f32[6,1,32,128]{3,0,2,1:T(8,128)S(1)}, u32[]{:S(2)}, u32[]{:S(2)}) collective-permute-start(f32[6,1,32,128]{3,0,2,1:T(8,128)} %get-tuple-element.62), channel_id=1, source_target_pairs={{0,32},{32,64},{64,96},{1,33},{33,65},{65,97},{2,34},{34,66},{66,9... | collective-permute-start | bytes 294920 | tf_op jit(solution)/shard_map/ppermute | solution.py:15
  19.2 23.2 %collective-permute-start.1 = (f32[6,1,32,128]{3,0,2,1:T(8,128)}, f32[6,1,32,128]{3,0,2,1:T(8,128)S(1)}, u32[]{:S(2)}, u32[]{:S(2)}) collective-permute-start(f32[6,1,32,128]{3,0,2,1:T(8,128)} %get-tuple-element.61), channel_id=1, source_target_pairs={{32,0},{64,32},{96,64},{33,1},{65,33},{97,65},{34,2},{66,34},{98,6... | collective-permute-start | bytes 294920 | tf_op jit(solution)/shard_map/ppermute | solution.py:17
  23.5 6.1 %collective-permute-start.4 = (f32[34,1,128]{2,0,1:T(8,128)S(1)}, f32[34,1,128]{2,0,1:T(8,128)S(1)}, u32[]{:S(2)}, u32[]{:S(2)}) collective-permute-start(f32[34,1,128]{2,0,1:T(8,128)S(1)} %copy.172), channel_id=1, source_target_pairs={{8,0},{16,8},{24,16},{9,1},{17,9},{25,17},{10,2},{18,10},{26,18},{... | collective-permute-start | bytes 52232 | tf_op jit(solution)/shard_map/ppermute | solution.py:17
  24.9 5.1 %collective-permute-start.6 = (f32[34,1,128]{2,0,1:T(8,128)S(1)}, f32[34,1,128]{2,0,1:T(8,128)S(1)}, u32[]{:S(2)}, u32[]{:S(2)}) collective-permute-start(f32[34,1,128]{2,0,1:T(8,128)S(1)} %copy.173), channel_id=1, source_target_pairs={{0,8},{8,16},{16,24},{1,9},{9,17},{17,25},{2,10},{10,18},{18,26},{... | collective-permute-start | bytes 52232 | tf_op jit(solution)/shard_map/ppermute | solution.py:15
  32.8 17.9 %collective-permute-start.8 = (f32[34,34,1]{1,0,2:T(8,128)S(1)}, f32[34,34,1]{1,0,2:T(8,128)S(1)}, u32[]{:S(2)}, u32[]{:S(2)}) collective-permute-start(f32[34,34,1]{1,0,2:T(8,128)S(1)} %copy.150), channel_id=1, source_target_pairs={{1,0},{2,1},{3,2},{4,3},{5,4},{6,5},{7,6},{9,8},{10,9},{11,10},{12... | collective-permute-start | bytes 13880 | tf_op jit(solution)/shard_map/ppermute | solution.py:17
  35.6 16.4 %collective-permute-start.10 = (f32[34,34,1]{1,0,2:T(8,128)S(1)}, f32[34,34,1]{1,0,2:T(8,128)S(1)}, u32[]{:S(2)}, u32[]{:S(2)}) collective-permute-start(f32[34,34,1]{1,0,2:T(8,128)S(1)} %copy.154), channel_id=1, source_target_pairs={{0,1},{1,2},{2,3},{3,4},{4,5},{5,6},{6,7},{8,9},{9,10},{10,11},{11... | collective-permute-start | bytes 13880 | tf_op jit(solution)/shard_map/ppermute | solution.py:15
  44.6 8.6 %collective-permute-start.5 = (f32[6,34,1,128]{3,0,2,1:T(8,128)S(1)}, f32[6,34,1,128]{3,0,2,1:T(8,128)S(1)}, u32[]{:S(2)}, u32[]{:S(2)}) collective-permute-start(f32[6,34,1,128]{3,0,2,1:T(8,128)S(1)} %get-tuple-element.56), channel_id=1, source_target_pairs={{8,0},{16,8},{24,16},{9,1},{17,9},{25,17},{10,2},{18,10},{26,18},{... | collective-permute-start | bytes 313352 | tf_op jit(solution)/shard_map/ppermute | solution.py:17
  45.9 7.4 %collective-permute-start.7 = (f32[6,34,1,128]{3,0,2,1:T(8,128)S(1)}, f32[6,34,1,128]{3,0,2,1:T(8,128)S(1)}, u32[]{:S(2)}, u32[]{:S(2)}) collective-permute-start(f32[6,34,1,128]{3,0,2,1:T(8,128)S(1)} %get-tuple-element.55), channel_id=1, source_target_pairs={{0,8},{8,16},{16,24},{1,9},{9,17},{17,25},{2,10},{10,18},{18,26},{... | collective-permute-start | bytes 313352 | tf_op jit(solution)/shard_map/ppermute | solution.py:15
  65.2 14.7 %collective-permute-start.9 = (f32[6,34,34,1]{2,3,1,0:T(1,128)}, f32[6,34,34,1]{2,3,1,0:T(1,128)}, u32[]{:S(2)}, u32[]{:S(2)}) collective-permute-start(f32[6,34,34,1]{2,3,1,0:T(1,128)} %copy.152), channel_id=1, source_target_pairs={{1,0},{2,1},{3,2},{4,3},{5,4},{6,5},{7,6},{9,8},{10,9},{11,10},{12... | collective-permute-start | bytes 83240 | tf_op jit(solution)/shard_map/ppermute | solution.py:17
  70.4 13.9 %collective-permute-start.11 = (f32[6,34,34,1]{2,3,1,0:T(1,128)}, f32[6,34,34,1]{2,3,1,0:T(1,128)}, u32[]{:S(2)}, u32[]{:S(2)}) collective-permute-start(f32[6,34,34,1]{2,3,1,0:T(1,128)} %copy.156), channel_id=1, source_target_pairs={{0,1},{1,2},{2,3},{3,4},{4,5},{5,6},{6,7},{8,9},{9,10},{10,11},{11... | collective-permute-start | bytes 83240 | tf_op jit(solution)/shard_map/ppermute | solution.py:15
  104.5 8.8 %collective-permute-start.12 = (f32[6,1,32,128]{3,0,2,1:T(8,128)S(1)}, f32[6,1,32,128]{3,0,2,1:T(8,128)S(1)}, u32[]{:S(2)}, u32[]{:S(2)}) collective-permute-start(f32[6,1,32,128]{3,0,2,1:T(8,128)S(1)} %get-tuple-element.60), channel_id=1, source_target_pairs={{32,0},{64,32},{96,64},{33,1},{65,33},{97,65},{34,2},{66,34},{98,6... | collective-permute-start | bytes 294920 | tf_op jit(solution)/shard_map/ppermute | solution.py:17
  107.7 6.8 %collective-permute-start.13 = (f32[6,1,32,128]{3,0,2,1:T(8,128)S(1)}, f32[6,1,32,128]{3,0,2,1:T(8,128)S(1)}, u32[]{:S(2)}, u32[]{:S(2)}) collective-permute-start(f32[6,1,32,128]{3,0,2,1:T(8,128)S(1)} %get-tuple-element.59), channel_id=1, source_target_pairs={{0,32},{32,64},{64,96},{1,33},{33,65},{65,97},{2,34},{34,66},{66,9... | collective-permute-start | bytes 294920 | tf_op jit(solution)/shard_map/ppermute | solution.py:15
  114.5 6.1 %collective-permute-start.14 = (f32[6,34,1,128]{3,0,2,1:T(8,128)S(1)}, f32[6,34,1,128]{3,0,2,1:T(8,128)S(1)}, u32[]{:S(2)}, u32[]{:S(2)}) collective-permute-start(f32[6,34,1,128]{3,0,2,1:T(8,128)S(1)} %get-tuple-element.54), channel_id=1, source_target_pairs={{8,0},{16,8},{24,16},{9,1},{17,9},{25,17},{10,2},{18,10},{26,18},{... | collective-permute-start | bytes 313352 | tf_op jit(solution)/shard_map/ppermute | solution.py:17
  115.8 6.3 %collective-permute-start.15 = (f32[6,34,1,128]{3,0,2,1:T(8,128)S(1)}, f32[6,34,1,128]{3,0,2,1:T(8,128)S(1)}, u32[]{:S(2)}, u32[]{:S(2)}) collective-permute-start(f32[6,34,1,128]{3,0,2,1:T(8,128)S(1)} %get-tuple-element.53), channel_id=1, source_target_pairs={{0,8},{8,16},{16,24},{1,9},{9,17},{17,25},{2,10},{10,18},{18,26},{... | collective-permute-start | bytes 313352 | tf_op jit(solution)/shard_map/ppermute | solution.py:15
  131.7 10.6 %collective-permute-start.16 = (f32[6,34,34,1]{2,3,1,0:T(1,128)S(1)}, f32[6,34,34,1]{2,3,1,0:T(1,128)}, u32[]{:S(2)}, u32[]{:S(2)}) collective-permute-start(f32[6,34,34,1]{2,3,1,0:T(1,128)S(1)} %copy.158), channel_id=1, source_target_pairs={{1,0},{2,1},{3,2},{4,3},{5,4},{6,5},{7,6},{9,8},{10,9},{11,10},{12... | collective-permute-start | bytes 83240 | tf_op jit(solution)/shard_map/ppermute | solution.py:17
  136.9 9.7 %collective-permute-start.17 = (f32[6,34,34,1]{2,3,1,0:T(1,128)}, f32[6,34,34,1]{2,3,1,0:T(1,128)}, u32[]{:S(2)}, u32[]{:S(2)}) collective-permute-start(f32[6,34,34,1]{2,3,1,0:T(1,128)} %copy.160), channel_id=1, source_target_pairs={{0,1},{1,2},{2,3},{3,4},{4,5},{5,6},{6,7},{8,9},{9,10},{10,11},{11... | collective-permute-start | bytes 83240 | tf_op jit(solution)/shard_map/ppermute | solution.py:15
  169.5 8.4 %collective-permute-start.18 = (f32[6,1,32,128]{3,0,2,1:T(8,128)S(1)}, f32[6,1,32,128]{3,0,2,1:T(8,128)S(1)}, u32[]{:S(2)}, u32[]{:S(2)}) collective-permute-start(f32[6,1,32,128]{3,0,2,1:T(8,128)S(1)} %get-tuple-element.58), channel_id=1, source_target_pairs={{32,0},{64,32},{96,64},{33,1},{65,33},{97,65},{34,2},{66,34},{98,6... | collective-permute-start | bytes 294920 | tf_op jit(solution)/shard_map/ppermute | solution.py:17
  171.4 7.7 %collective-permute-start.19 = (f32[6,1,32,128]{3,0,2,1:T(8,128)S(1)}, f32[6,1,32,128]{3,0,2,1:T(8,128)S(1)}, u32[]{:S(2)}, u32[]{:S(2)}) collective-permute-start(f32[6,1,32,128]{3,0,2,1:T(8,128)S(1)} %get-tuple-element.57), channel_id=1, source_target_pairs={{0,32},{32,64},{64,96},{1,33},{33,65},{65,97},{2,34},{34,66},{66,9... | collective-permute-start | bytes 294920 | tf_op jit(solution)/shard_map/ppermute | solution.py:15
  179.2 6.6 %collective-permute-start.20 = (f32[6,34,1,128]{3,0,2,1:T(8,128)S(1)}, f32[6,34,1,128]{3,0,2,1:T(8,128)S(1)}, u32[]{:S(2)}, u32[]{:S(2)}) collective-permute-start(f32[6,34,1,128]{3,0,2,1:T(8,128)S(1)} %get-tuple-element.52), channel_id=1, source_target_pairs={{8,0},{16,8},{24,16},{9,1},{17,9},{25,17},{10,2},{18,10},{26,18},{... | collective-permute-start | bytes 313352 | tf_op jit(solution)/shard_map/ppermute | solution.py:17
  180.5 6.7 %collective-permute-start.21 = (f32[6,34,1,128]{3,0,2,1:T(8,128)S(1)}, f32[6,34,1,128]{3,0,2,1:T(8,128)S(1)}, u32[]{:S(2)}, u32[]{:S(2)}) collective-permute-start(f32[6,34,1,128]{3,0,2,1:T(8,128)S(1)} %get-tuple-element.51), channel_id=1, source_target_pairs={{0,8},{8,16},{16,24},{1,9},{9,17},{17,25},{2,10},{10,18},{18,26},{... | collective-permute-start | bytes 313352 | tf_op jit(solution)/shard_map/ppermute | solution.py:15
  196.8 10.0 %collective-permute-start.22 = (f32[6,34,34,1]{2,3,1,0:T(1,128)S(1)}, f32[6,34,34,1]{2,3,1,0:T(1,128)S(1)}, u32[]{:S(2)}, u32[]{:S(2)}) collective-permute-start(f32[6,34,34,1]{2,3,1,0:T(1,128)S(1)} %copy.162), channel_id=1, source_target_pairs={{1,0},{2,1},{3,2},{4,3},{5,4},{6,5},{7,6},{9,8},{10,9},{11,10},{12... | collective-permute-start | bytes 83240 | tf_op jit(solution)/shard_map/ppermute | solution.py:17
  201.4 9.0 %collective-permute-start.23 = (f32[6,34,34,1]{2,3,1,0:T(1,128)S(1)}, f32[6,34,34,1]{2,3,1,0:T(1,128)S(1)}, u32[]{:S(2)}, u32[]{:S(2)}) collective-permute-start(f32[6,34,34,1]{2,3,1,0:T(1,128)S(1)} %copy.164), channel_id=1, source_target_pairs={{0,1},{1,2},{2,3},{3,4},{4,5},{5,6},{6,7},{8,9},{9,10},{10,11},{11... | collective-permute-start | bytes 83240 | tf_op jit(solution)/shard_map/ppermute | solution.py:15
  (45 other events, 2502.9 us)
where the time goes:
time: 487 us; the launch traced here: 478 us
  local copies, waits for them, and re-layouts  157 us (32%)
  blocking collectives  83.5 us (17%)
  other arithmetic  78 us (16%)
  starting transfers between devices  74.1 us (15%)
  matrix products  60.5 us (12%)
  between operations  18.3 us (4%)
  waiting for transfers between devices  6 us (1%)
    psum x1, blocking collectives, on_device(): total_gram = lax.psum(gram, ('gx', 'gy', 'gz'))  83.5 us
    unnamed x100, local copies, waits for them, and re-layouts  58.9 us
    ppermute x12, starting transfers between devices, extended(): lax.ppermute(tail, axis, [(i, (i + 1) % count) for i in range(ends)])  54.8 us
    div x3, other arithmetic, stencil(): return 2.5 * accum / diagonal  53.5 us
    slice x9, local copies, waits for them, and re-layouts, extended(): head = lax.slice_in_dim(cells, 0, width, axis=dim)  29.1 us
    dot_general x1, matrix products, on_device(): solved = jnp.dot(inverse, flat, precision=lax.Precision.HIGHEST)  24.5 us
    dot_general x24, matrix products, lower_inverse(): jnp.dot(lower[row_index], inverse, precision=lax.Precision.HIGHEST)  19.6 us
    ppermute x12, starting transfers between devices, extended(): lax.ppermute(head, axis, [((i + 1) % count, i) for i in range(ends)])  19.3 us
  transfers between devices with their start and end apart: 24, of which 8 were waited for; matrix products, arithmetic and copies ran while one was open for 10% of the time, Pallas kernels for 0%

commit v1 on v0

--- a/solution.py
+++ b/solution.py
@@ -99,7 +99,7 @@
     flat = basis.reshape(columns, -1)
     cell_count = flat.shape[1] * lax.axis_size("gx") * lax.axis_size("gy") * lax.axis_size("gz")
     gram = jnp.dot(flat, flat.T, precision=lax.Precision.HIGHEST)
-    total_gram = lax.psum(gram, ("gx", "gy", "gz"))
+    total_gram = lax.psum(lax.psum(gram, "gx"), ("gy", "gz"))
     factor_r = lower_factor(total_gram / cell_count).T
     inverse = lower_inverse(factor_r.T)
     solved = jnp.dot(inverse, flat, precision=lax.Precision.HIGHEST)

time: 487 us -> 605 us (1.24)
  the two profiles are of different devices: /device:TPU:1 before, /device:TPU:8 now
where the time goes in v1:
time: 605 us; the launch traced here: 595 us
  blocking collectives  198 us (33%)
  local copies, waits for them, and re-layouts  157 us (26%)
  other arithmetic  79.4 us (13%)
  starting transfers between devices  69.7 us (12%)
  matrix products  60.5 us (10%)
  between operations  18.5 us (3%)
  waiting for transfers between devices  11.5 us (2%)
    psum x2, blocking collectives, on_device(): total_gram = lax.psum(lax.psum(gram, 'gx'), ('gy', 'gz'))  198 us
    unnamed x100, local copies, waits for them, and re-layouts  58.9 us
    div x3, other arithmetic, stencil(): return 2.5 * accum / diagonal  55 us
    ppermute x12, starting transfers between devices, extended(): lax.ppermute(tail, axis, [(i, (i + 1) % count) for i in range(ends)])  48.3 us
    slice x9, local copies, waits for them, and re-layouts, extended(): head = lax.slice_in_dim(cells, 0, width, axis=dim)  29.1 us
    dot_general x1, matrix products, on_device(): solved = jnp.dot(inverse, flat, precision=lax.Precision.HIGHEST)  24.5 us
    ppermute x12, starting transfers between devices, extended(): lax.ppermute(head, axis, [((i + 1) % count, i) for i in range(ends)])  21.4 us
    dot_general x24, matrix products, lower_inverse(): jnp.dot(lower[row_index], inverse, precision=lax.Precision.HIGHEST)  19.6 us
  transfers between devices with their start and end apart: 24, of which 7 were waited for; matrix products, arithmetic and copies ran while one was open for 8% of the time, Pallas kernels for 0%

profile of v1, /device:TPU:8, one launch (start us, length us, event | category | flops | bytes accessed | tf_op | source)
XLA Modules:
  0.0 595.2 jit_solution(3977242869494724263)
XLA Ops:
  7.0 4.7 copy.166
  46.4 4.8 collective-permute-start.7
  57.0 5.2 fusion.259
  71.3 5.3 collective-permute-start.11
  76.7 4.6 compare_select_fusion
  90.1 16.2 %fusion.31 = f32[6,32,32,128]{3,0,2,1:T(8,128)S(1)} fusion(f32[6,34,34,1]{3,0,2,1:T(8,128)} %copy.157, f32[6,34,1,128]{3,0,2,1:T(8,128)S(1)} %collective-permute-done.5, f32[6,34,32,128]{3,0,2,1:T(8,128)} %copy-done.6, f32[6,34,1,128]{3,0,2,1:T(8,128)S(1)} %collective-permute-done.7, f32[6,34,34,1]{3,0,2,1:T(8,128)} %copy.153, ...), kind=kLoop, calls=%fused_computation.73 | loop fusion | flops 18087936 | bytes 13764800 | tf_op jit(solution)/shard_map/div | solution.py:58
  115.9 4.6 collective-permute-start.15
  124.1 5.2 fusion.258
  137.8 5.4 collective-permute-start.17
  152.4 18.6 %fusion.18 = f32[6,32,32,128]{3,0,2,1:T(8,128)S(1)} fusion(f32[6,34,34,1]{3,0,2,1:T(8,128)} %copy.161, f32[6,34,1,128]{3,0,2,1:T(8,128)} %copy-done.14, f32[6,34,1,128]{3,0,2,1:T(8,128)} %copy-done.16, f32[6,1,32,128]{3,0,2,1:T(8,128)S(1)} %collective-permute-done.12, f32[6,32,32,128]{3,0,2,1:T(8,128)} %copy-done.1, ...), kind=kLoop, calls=%fused_computation.42 | loop fusion | flops 24379392 | bytes 10422464 | tf_op jit(solution)/shard_map/div | solution.py:58
  180.6 5.0 collective-permute-start.21
  189.3 5.2 fusion.257
  202.4 5.3 collective-permute-start.23
  215.4 20.2 %fusion.5 = f32[6,32,32,128]{3,0,2,1:T(8,128)} fusion(f32[6,34,34,1]{3,0,2,1:T(8,128)} %copy.165, f32[6,34,1,128]{3,0,2,1:T(8,128)} %copy-done.13, f32[6,34,1,128]{3,0,2,1:T(8,128)} %copy-done.15, f32[6,1,32,128]{3,0,2,1:T(8,128)} %copy-done.11, f32[6,32,32,128]{3,0,2,1:T(8,128)} %copy-done.3, f32[6,1,32,128]{3,0,2,1:T(8,128)} %copy-done.12, ...), kind=kLoop, calls=%fused_computation.11 | loop fusion | flops 24379392 | bytes 10422464 | tf_op jit(solution)/shard_map/div | solution.py:58
  235.6 6.2 %pad_maximum_fusion = f32[24,32,32,128]{3,0,2,1:T(8,128)S(1)} fusion(f32[6,32,32,128]{3,0,2,1:T(8,128)} %fusion.5, f32[6,32,32,128]{3,0,2,1:T(8,128)S(1)} %copy-done.4, f32[6,32,32,128]{3,0,2,1:T(8,128)S(1)} %copy-done.2, f32[6,32,32,128]{3,0,2,1:T(8,128)} %copy-done.5), kind=kLoop, calls=%fused_computation.1 | loop fusion | flops 9437184 | bytes 25165824 | tf_op jit(solution)/shard_map/concatenate | solution.py:97
  241.8 4.8 copy-done
  246.7 13.1 %convolution_bitcast_fusion = f32[24,24]{1,0:T(8,128)S(1)} fusion(f32[24,32,32,128]{3,0,2,1:T(8,128)S(1)} %pad_maximum_fusion), kind=kOutput, calls=%fused_computation.99 | convolution fusion | flops 905969664 | bytes 12585216 | tf_op jit(solution)/shard_map/dot_general | solution.py:101
  259.8 10.1 %psum.14 = f32[24,24]{1,0:T(8,128)S(1)} all-reduce(f32[24,24]{1,0:T(8,128)S(1)} %convolution_bitcast_fusion), channel_id=1, replica_groups=mesh['gx'=4,'gy'=4,'gz'=8] {'gx'}, use_global_device_ids=true, to_apply=%region_0.1 | all-reduce | flops 576 | bytes 4608 | tf_op jit(solution)/shard_map/psum | solution.py:102
  269.9 188.1 %psum.15 = f32[24,24]{1,0:T(8,128)S(1)} all-reduce(f32[24,24]{1,0:T(8,128)S(1)} %psum.14), channel_id=1, replica_groups=mesh['gx'=4,'gy'=4,'gz'=8] {'gy','gz'}, use_global_device_ids=true, to_apply=%region_1.2 | all-reduce | flops 576 | bytes 4608 | tf_op jit(solution)/shard_map/psum | solution.py:102
  498.9 11.5 %copy.167 = f32[24,32,32,128]{3,2,1,0:T(8,128)} copy(f32[24,32,32,128]{3,0,2,1:T(8,128)} %copy-done) | data formatting | bytes 25165824 | tf_op jit(solution)/shard_map/concatenate | solution.py:97
  527.2 16.8 %copy.180 = f32[3,8,1024,128]{3,1,2,0:T(8,128)} copy(f32[3,8,1024,128]{3,2,1,0:T(8,128)} %bitcast.525) | data formatting | bytes 25165824
  544.0 11.3 %copy.175 = f32[3,8,1024,128]{3,2,1,0:T(8,128)} copy(f32[3,8,1024,128]{3,1,2,0:T(8,128)} %copy.180) | data formatting | bytes 25165824
  558.5 24.5 %fusion = f32[24,32,32,128]{3,0,2,1:T(8,128)} fusion(f32[32,32,128,24]{2,1,0,3:T(8,128)} %bitcast.526, f32[24,24]{1,0:T(8,128)S(1)} %multiply_add_fusion.5, f32[24]{0:T(128)S(1)} %fusion.112, f32[24]{0:T(128)S(1)} %copy-done.44, f32[24]{0:T(128)S(1)} %fusion.111, f32[24]{0:T(128)S(1)} %copy-done.43, f32[24]{0:T(128)S(1)} %fusion.110, f32[24]{0:T(128)S(1)} %copy-done.42, ...), kind=kOutput, calls=%fused_computation.2 | convolution fusion | flops 905974272 | bytes 25168896 | tf_op jit(solution)/shard_map/dot_general | solution.py:105
  583.0 11.8 %copy.169 = f32[24,32,32,128]{3,2,1,0:T(8,128)} copy(f32[24,32,32,128]{3,0,2,1:T(8,128)} %fusion) | data formatting | bytes 25165824
  (311 shorter events, 168.1 us)
Async XLA Ops:
  1.4 19.9 %collective-permute-start.2 = (f32[1,32,128]{2,1,0:T(8,128)S(1)}, f32[1,32,128]{2,1,0:T(8,128)S(1)}, u32[]{:S(2)}, u32[]{:S(2)}) collective-permute-start(f32[1,32,128]{2,1,0:T(8,128)S(1)} %get-tuple-element.68), channel_id=1, source_target_pairs={{0,32},{32,64},{64,96},{1,33},{33,65},{65,97},{2,34},{34,66},{66,9... | collective-permute-start | bytes 49160 | tf_op jit(solution)/shard_map/ppermute | solution.py:15
  3.4 18.0 %collective-permute-start = (f32[1,32,128]{2,1,0:T(8,128)S(1)}, f32[1,32,128]{2,1,0:T(8,128)S(1)}, u32[]{:S(2)}, u32[]{:S(2)}) collective-permute-start(f32[1,32,128]{2,1,0:T(8,128)S(1)} %get-tuple-element.67), channel_id=1, source_target_pairs={{32,0},{64,32},{96,64},{33,1},{65,33},{97,65},{34,2},{66,34},{98,6... | collective-permute-start | bytes 49160 | tf_op jit(solution)/shard_map/ppermute | solution.py:17
  14.4 25.6 %collective-permute-start.3 = (f32[6,1,32,128]{3,0,2,1:T(8,128)}, f32[6,1,32,128]{3,0,2,1:T(8,128)S(1)}, u32[]{:S(2)}, u32[]{:S(2)}) collective-permute-start(f32[6,1,32,128]{3,0,2,1:T(8,128)} %get-tuple-element.62), channel_id=1, source_target_pairs={{0,32},{32,64},{64,96},{1,33},{33,65},{65,97},{2,34},{34,66},{66,9... | collective-permute-start | bytes 294920 | tf_op jit(solution)/shard_map/ppermute | solution.py:15
  16.5 26.4 %collective-permute-start.1 = (f32[6,1,32,128]{3,0,2,1:T(8,128)}, f32[6,1,32,128]{3,0,2,1:T(8,128)S(1)}, u32[]{:S(2)}, u32[]{:S(2)}) collective-permute-start(f32[6,1,32,128]{3,0,2,1:T(8,128)} %get-tuple-element.61), channel_id=1, source_target_pairs={{32,0},{64,32},{96,64},{33,1},{65,33},{97,65},{34,2},{66,34},{98,6... | collective-permute-start | bytes 294920 | tf_op jit(solution)/shard_map/ppermute | solution.py:17
  22.5 6.4 %collective-permute-start.4 = (f32[34,1,128]{2,0,1:T(8,128)S(1)}, f32[34,1,128]{2,0,1:T(8,128)S(1)}, u32[]{:S(2)}, u32[]{:S(2)}) collective-permute-start(f32[34,1,128]{2,0,1:T(8,128)S(1)} %copy.172), channel_id=1, source_target_pairs={{8,0},{16,8},{24,16},{9,1},{17,9},{25,17},{10,2},{18,10},{26,18},{... | collective-permute-start | bytes 52232 | tf_op jit(solution)/shard_map/ppermute | solution.py:17
  23.9 6.0 %collective-permute-start.6 = (f32[34,1,128]{2,0,1:T(8,128)S(1)}, f32[34,1,128]{2,0,1:T(8,128)S(1)}, u32[]{:S(2)}, u32[]{:S(2)}) collective-permute-start(f32[34,1,128]{2,0,1:T(8,128)S(1)} %copy.173), channel_id=1, source_target_pairs={{0,8},{8,16},{16,24},{1,9},{9,17},{17,25},{2,10},{10,18},{18,26},{... | collective-permute-start | bytes 52232 | tf_op jit(solution)/shard_map/ppermute | solution.py:15
  32.8 19.1 %collective-permute-start.8 = (f32[34,34,1]{1,0,2:T(8,128)S(1)}, f32[34,34,1]{1,0,2:T(8,128)S(1)}, u32[]{:S(2)}, u32[]{:S(2)}) collective-permute-start(f32[34,34,1]{1,0,2:T(8,128)S(1)} %copy.150), channel_id=1, source_target_pairs={{1,0},{2,1},{3,2},{4,3},{5,4},{6,5},{7,6},{9,8},{10,9},{11,10},{12... | collective-permute-start | bytes 13880 | tf_op jit(solution)/shard_map/ppermute | solution.py:17
  35.5 17.5 %collective-permute-start.10 = (f32[34,34,1]{1,0,2:T(8,128)S(1)}, f32[34,34,1]{1,0,2:T(8,128)S(1)}, u32[]{:S(2)}, u32[]{:S(2)}) collective-permute-start(f32[34,34,1]{1,0,2:T(8,128)S(1)} %copy.154), channel_id=1, source_target_pairs={{0,1},{1,2},{2,3},{3,4},{4,5},{5,6},{6,7},{8,9},{9,10},{10,11},{11... | collective-permute-start | bytes 13880 | tf_op jit(solution)/shard_map/ppermute | solution.py:15
  45.1 9.2 %collective-permute-start.5 = (f32[6,34,1,128]{3,0,2,1:T(8,128)S(1)}, f32[6,34,1,128]{3,0,2,1:T(8,128)S(1)}, u32[]{:S(2)}, u32[]{:S(2)}) collective-permute-start(f32[6,34,1,128]{3,0,2,1:T(8,128)S(1)} %get-tuple-element.56), channel_id=1, source_target_pairs={{8,0},{16,8},{24,16},{9,1},{17,9},{25,17},{10,2},{18,10},{26,18},{... | collective-permute-start | bytes 313352 | tf_op jit(solution)/shard_map/ppermute | solution.py:17
  46.4 7.9 %collective-permute-start.7 = (f32[6,34,1,128]{3,0,2,1:T(8,128)S(1)}, f32[6,34,1,128]{3,0,2,1:T(8,128)S(1)}, u32[]{:S(2)}, u32[]{:S(2)}) collective-permute-start(f32[6,34,1,128]{3,0,2,1:T(8,128)S(1)} %get-tuple-element.55), channel_id=1, source_target_pairs={{0,8},{8,16},{16,24},{1,9},{9,17},{17,25},{2,10},{10,18},{18,26},{... | collective-permute-start | bytes 313352 | tf_op jit(solution)/shard_map/ppermute | solution.py:15
  66.1 15.2 %collective-permute-start.9 = (f32[6,34,34,1]{2,3,1,0:T(1,128)}, f32[6,34,34,1]{2,3,1,0:T(1,128)}, u32[]{:S(2)}, u32[]{:S(2)}) collective-permute-start(f32[6,34,34,1]{2,3,1,0:T(1,128)} %copy.152), channel_id=1, source_target_pairs={{1,0},{2,1},{3,2},{4,3},{5,4},{6,5},{7,6},{9,8},{10,9},{11,10},{12... | collective-permute-start | bytes 83240 | tf_op jit(solution)/shard_map/ppermute | solution.py:17
  71.3 14.4 %collective-permute-start.11 = (f32[6,34,34,1]{2,3,1,0:T(1,128)}, f32[6,34,34,1]{2,3,1,0:T(1,128)}, u32[]{:S(2)}, u32[]{:S(2)}) collective-permute-start(f32[6,34,34,1]{2,3,1,0:T(1,128)} %copy.156), channel_id=1, source_target_pairs={{0,1},{1,2},{2,3},{3,4},{4,5},{5,6},{6,7},{8,9},{9,10},{10,11},{11... | collective-permute-start | bytes 83240 | tf_op jit(solution)/shard_map/ppermute | solution.py:15
  106.3 4.9 collective-permute-start.12
  108.2 6.3 %collective-permute-start.13 = (f32[6,1,32,128]{3,0,2,1:T(8,128)S(1)}, f32[6,1,32,128]{3,0,2,1:T(8,128)S(1)}, u32[]{:S(2)}, u32[]{:S(2)}) collective-permute-start(f32[6,1,32,128]{3,0,2,1:T(8,128)S(1)} %get-tuple-element.59), channel_id=1, source_target_pairs={{0,32},{32,64},{64,96},{1,33},{33,65},{65,97},{2,34},{34,66},{66,9... | collective-permute-start | bytes 294920 | tf_op jit(solution)/shard_map/ppermute | solution.py:15
  114.6 6.9 %collective-permute-start.14 = (f32[6,34,1,128]{3,0,2,1:T(8,128)S(1)}, f32[6,34,1,128]{3,0,2,1:T(8,128)S(1)}, u32[]{:S(2)}, u32[]{:S(2)}) collective-permute-start(f32[6,34,1,128]{3,0,2,1:T(8,128)S(1)} %get-tuple-element.54), channel_id=1, source_target_pairs={{8,0},{16,8},{24,16},{9,1},{17,9},{25,17},{10,2},{18,10},{26,18},{... | collective-permute-start | bytes 313352 | tf_op jit(solution)/shard_map/ppermute | solution.py:17
  115.9 7.1 %collective-permute-start.15 = (f32[6,34,1,128]{3,0,2,1:T(8,128)S(1)}, f32[6,34,1,128]{3,0,2,1:T(8,128)S(1)}, u32[]{:S(2)}, u32[]{:S(2)}) collective-permute-start(f32[6,34,1,128]{3,0,2,1:T(8,128)S(1)} %get-tuple-element.53), channel_id=1, source_target_pairs={{0,8},{8,16},{16,24},{1,9},{9,17},{17,25},{2,10},{10,18},{18,26},{... | collective-permute-start | bytes 313352 | tf_op jit(solution)/shard_map/ppermute | solution.py:15
  132.6 11.1 %collective-permute-start.16 = (f32[6,34,34,1]{2,3,1,0:T(1,128)S(1)}, f32[6,34,34,1]{2,3,1,0:T(1,128)}, u32[]{:S(2)}, u32[]{:S(2)}) collective-permute-start(f32[6,34,34,1]{2,3,1,0:T(1,128)S(1)} %copy.158), channel_id=1, source_target_pairs={{1,0},{2,1},{3,2},{4,3},{5,4},{6,5},{7,6},{9,8},{10,9},{11,10},{12... | collective-permute-start | bytes 83240 | tf_op jit(solution)/shard_map/ppermute | solution.py:17
  137.8 10.3 %collective-permute-start.17 = (f32[6,34,34,1]{2,3,1,0:T(1,128)}, f32[6,34,34,1]{2,3,1,0:T(1,128)}, u32[]{:S(2)}, u32[]{:S(2)}) collective-permute-start(f32[6,34,34,1]{2,3,1,0:T(1,128)} %copy.160), channel_id=1, source_target_pairs={{0,1},{1,2},{2,3},{3,4},{4,5},{5,6},{6,7},{8,9},{9,10},{10,11},{11... | collective-permute-start | bytes 83240 | tf_op jit(solution)/shard_map/ppermute | solution.py:15
  171.1 4.9 collective-permute-start.18
  173.0 6.3 %collective-permute-start.19 = (f32[6,1,32,128]{3,0,2,1:T(8,128)S(1)}, f32[6,1,32,128]{3,0,2,1:T(8,128)S(1)}, u32[]{:S(2)}, u32[]{:S(2)}) collective-permute-start(f32[6,1,32,128]{3,0,2,1:T(8,128)S(1)} %get-tuple-element.57), channel_id=1, source_target_pairs={{0,32},{32,64},{64,96},{1,33},{33,65},{65,97},{2,34},{34,66},{66,9... | collective-permute-start | bytes 294920 | tf_op jit(solution)/shard_map/ppermute | solution.py:15
  179.3 7.4 %collective-permute-start.20 = (f32[6,34,1,128]{3,0,2,1:T(8,128)S(1)}, f32[6,34,1,128]{3,0,2,1:T(8,128)S(1)}, u32[]{:S(2)}, u32[]{:S(2)}) collective-permute-start(f32[6,34,1,128]{3,0,2,1:T(8,128)S(1)} %get-tuple-element.52), channel_id=1, source_target_pairs={{8,0},{16,8},{24,16},{9,1},{17,9},{25,17},{10,2},{18,10},{26,18},{... | collective-permute-start | bytes 313352 | tf_op jit(solution)/shard_map/ppermute | solution.py:17
  180.6 7.6 %collective-permute-start.21 = (f32[6,34,1,128]{3,0,2,1:T(8,128)S(1)}, f32[6,34,1,128]{3,0,2,1:T(8,128)S(1)}, u32[]{:S(2)}, u32[]{:S(2)}) collective-permute-start(f32[6,34,1,128]{3,0,2,1:T(8,128)S(1)} %get-tuple-element.51), channel_id=1, source_target_pairs={{0,8},{8,16},{16,24},{1,9},{9,17},{17,25},{2,10},{10,18},{18,26},{... | collective-permute-start | bytes 313352 | tf_op jit(solution)/shard_map/ppermute | solution.py:15
  197.8 10.5 %collective-permute-start.22 = (f32[6,34,34,1]{2,3,1,0:T(1,128)S(1)}, f32[6,34,34,1]{2,3,1,0:T(1,128)S(1)}, u32[]{:S(2)}, u32[]{:S(2)}) collective-permute-start(f32[6,34,34,1]{2,3,1,0:T(1,128)S(1)} %copy.162), channel_id=1, source_target_pairs={{1,0},{2,1},{3,2},{4,3},{5,4},{6,5},{7,6},{9,8},{10,9},{11,10},{12... | collective-permute-start | bytes 83240 | tf_op jit(solution)/shard_map/ppermute | solution.py:17
  202.4 9.5 %collective-permute-start.23 = (f32[6,34,34,1]{2,3,1,0:T(1,128)S(1)}, f32[6,34,34,1]{2,3,1,0:T(1,128)S(1)}, u32[]{:S(2)}, u32[]{:S(2)}) collective-permute-start(f32[6,34,34,1]{2,3,1,0:T(1,128)S(1)} %copy.164), channel_id=1, source_target_pairs={{0,1},{1,2},{2,3},{3,4},{4,5},{5,6},{6,7},{8,9},{9,10},{10,11},{11... | collective-permute-start | bytes 83240 | tf_op jit(solution)/shard_map/ppermute | solution.py:15
  (45 other events, 4587.7 us)
